TPU v7x, 1024 devices: a whole 4x4x32 slice. The times are simulated.
1024 devices in a mesh: rep: 128 (over y_lo, z, core), fsdp: 8 (over x, y_hi).
Axes of the slice: x: 4, y: 4 (y_hi: 2, y_lo: 2; y = y_hi * 2 + y_lo), z: 32, core: 2. Of those that a mesh axis runs over, the one named last changes fastest.
Arguments:
- tokens: bfloat16 [229376, 6144], P(('rep', 'fsdp')), may hold values from -6 to 6
- query_weight: bfloat16 [128, 6144, 128], P('rep', 'fsdp'), may hold values from -0.078125 to 0.078125
- global_params: float32 [6144, 256], P('fsdp'), may hold values from -6 to 6
- local_params: bfloat16 [128, 6144, 256], P('rep', 'fsdp'), may hold values from -24 to 24
- momentum: float32 [8, 6144, 256], P(None, ('fsdp', 'rep')), may hold values from -0.6 to 0.6
- inner_steps: int32 [128], replicated, may hold values from 20 to 100
- replica_tokens: int32 [128], replicated, may hold values from 100000 to 400000
- plan: int32 [1], replicated, may hold values from 0 to 7
Outputs:
- queries: bfloat16 [229376, 128], P(('rep', 'fsdp'))
- new_params: float32 [6144, 256], P('fsdp')
- new_momentum: float32 [6144, 256], P(('fsdp', 'rep'))
All inputs are finite; a program needn't handle non-finite values. Where the computation divides by a largest or mean magnitude, that divisor is 1e-20 or more.
Results may differ from a plain program's by a relative error of at most 0.0028.
Values may be sent and summed in bfloat16 or wider, within the bound.
A program may use at most 32 MiB of HBM per device.

v0:
```python
import math

import jax
import jax.numpy as jnp
from jax import lax
from jax.sharding import PartitionSpec as P

BLOCK = 128


decay_rate = 0.9
outer_rate = 0.7


def hadamard_table(order_n):
    row_ids = lax.broadcasted_iota(jnp.int32, (order_n, order_n), 0)
    col_ids = lax.broadcasted_iota(jnp.int32, (order_n, order_n), 1)
    common = jnp.bitwise_and(row_ids, col_ids)
    parity = jnp.zeros((order_n, order_n), jnp.int32)
    for bit_pos in range(order_n.bit_length() - 1):
        parity = parity + jnp.bitwise_and(jnp.right_shift(common, bit_pos), 1)
    signs = 1 - 2 * jnp.bitwise_and(parity, 1)
    return signs.astype(jnp.float32) / math.sqrt(order_n)


def rotate_blocks(matrix, table):
    row_count = matrix.shape[0]
    blocks = matrix.reshape(row_count, matrix.shape[1] // BLOCK, BLOCK)
    return jnp.einsum("rkb,bc->rkc", blocks, table, precision=lax.Precision.HIGHEST)


def local(
    tokens, query_weight, global_params, local_params, momentum, inner_steps, replica_tokens, plan
):
    replica = lax.axis_index("rep")
    ratio = replica_tokens.astype(jnp.float32) / inner_steps.astype(jnp.float32)
    weight_mine = lax.dynamic_index_in_dim(ratio, replica, 0, keepdims=False) / jnp.sum(ratio)
    table = hadamard_table(BLOCK)
    shard_rows = global_params.shape[0]
    delta = global_params - local_params[0].astype(jnp.float32)
    rotated = rotate_blocks(delta, table)
    scale = jnp.max(jnp.abs(rotated), axis=-1, keepdims=True) + 1e-06
    code = lax.optimization_barrier((rotated / scale).astype(jnp.bfloat16))
    term = (code.astype(jnp.float32) * scale * weight_mine).reshape(
        shard_rows, global_params.shape[1]
    )
    queries = jnp.dot(
        tokens,
        lax.all_gather(query_weight, "fsdp", axis=1, tiled=True)[0],
        preferred_element_type=jnp.float32,
    ).astype(jnp.bfloat16)
    slot = lax.dynamic_index_in_dim(momentum, plan[0], 0, keepdims=False)
    owned_rows = slot.shape[0]
    summed = lax.psum(term, "rep")
    average = rotate_blocks(summed, table).reshape(shard_rows, term.shape[1])
    slot_full = lax.all_gather(slot, "rep", axis=0, tiled=True)
    momentum_full = decay_rate * slot_full + average
    new_params = global_params - outer_rate * (average + decay_rate * momentum_full)
    new_momentum = lax.dynamic_slice_in_dim(momentum_full, replica * owned_rows, owned_rows, 0)
    return (queries, new_params, new_momentum)


def solution(mesh):
    return jax.shard_map(
        local,
        mesh=mesh,
        in_specs=(
            P(("rep", "fsdp"), None),
            P("rep", "fsdp", None),
            P("fsdp", None),
            P("rep", "fsdp", None),
            P(None, ("fsdp", "rep"), None),
            P(),
            P(),
            P(),
        ),
        out_specs=(P(("rep", "fsdp"), None), P("fsdp", None), P(("fsdp", "rep"), None)),
        check_vma=False,
    )
```

profile of v0, /device:TPU:1, one launch (start us, length us, event | category | flops | bytes accessed | tf_op | source)
XLA Modules:
  0.0 846.8 jit_solution(9318326466272923806)
XLA Ops:
  8.0 0.0 copy-start
  8.0 0.0 copy-start.1
  8.0 0.0 copy-start.2
  8.0 0.0 all-reduce.2.cloned.1.call-start
  8.1 2.3 abs_reduce_fusion
  10.4 0.1 divide_convert_fusion
  10.5 0.0 copy-done.1
  10.5 0.0 copy-done.2
  10.5 0.6 fusion.28
  11.1 0.6 dynamic_slice.11
  13.1 1.0 multiply_multiply_fusion
  14.0 0.0 all-reduce.2.cloned.1.call-update
  14.0 0.0 all-gather.3.cloned.1.call-start
  14.1 0.5 all-gather.3.cloned.1.call-update
  15.3 0.8 constant_dynamic-slice_fusion.1
  16.1 138.2 %all-gather = f32[1,768,256]{2,0,1:T(1,128)S(1)} all-gather(f32[1,6,256]{2,0,1:T(1,128)S(1)} %constant_dynamic-slice_fusion.1), channel_id=2, replica_groups=mesh['rep'=128,'fsdp'=8] {'rep'}, dimensions={1}, use_global_device_ids=true | all-gather | bytes 792576 | tf_op jit(solution)/shard_map/all_gather | solution.py:56
  154.3 1.7 broadcast_multiply_fusion
  156.0 674.1 %all-reduce.2.cloned.1.call-done = f32[768,2,128]{0,2,1:T(8,128)} async-done(((f32[768,2,128]{0,2,1:T(8,128)}), f32[768,2,128]{0,2,1:T(8,128)}) %all-reduce.2.cloned.1.call-update) | async-done | bytes 786448 | tf_op jit(solution)/shard_map/psum | solution.py:54
  830.1 2.0 fusion.9
  832.1 1.1 copy.19
  833.2 2.7 multiply_subtract_fusion
  835.9 0.6 constant_dynamic-slice_fusion
  836.5 0.0 all-gather.3.cloned.1.call-done
  836.5 0.0 copy-done
  836.5 2.9 fusion.2
  (1 shorter events, 0.0 us)
Async XLA Ops:
  8.0 828.5 %copy-start = (bf16[224,6144]{1,0:T(8,128)(2,1)S(1)}, bf16[224,6144]{1,0:T(8,128)(2,1)}, u32[]{:S(2)}) copy-start(bf16[224,6144]{1,0:T(8,128)(2,1)} %param.8) | copy-start | bytes 8257540
  8.0 2.5 copy-start.1
  8.0 2.5 copy-start.2
  8.0 822.0 %all-reduce.2.cloned.1.call-start = ((), (), s32[]{:S(2)}) async-start(), calls=%async_computation.1 | async-start | bytes 1572864 | tf_op jit(solution)/shard_map/psum | solution.py:54
  14.0 822.4 %all-gather.3.cloned.1.call-start = ((), (), s32[]{:S(2)}) async-start(), calls=%async_computation | async-start | bytes 1769472 | tf_op jit(solution)/shard_map/all_gather | solution.py:49
Sparse Core Ops, SparseCore 0:
  14.2 815.8 all-reduce.1
Sparse Core Ops, SparseCore 1:
  18.9 94.2 all-gather.2
where the time goes:
time: 848 us; the launch traced here: 847 us
  waiting for transfers between devices  675 us (80%)
  blocking collectives  138 us (16%)
  between operations  17.5 us (2%)
    psum x1, waiting for transfers between devices, local(): summed = lax.psum(term, 'rep')  674 us
    all_gather x1, blocking collectives, local(): slot_full = lax.all_gather(slot, 'rep', axis=0, tiled=True)  138 us
  transfers between devices with their start and end apart: 2, of which 1 were waited for; matrix products, arithmetic and copies ran while one was open for 1% of the time, Pallas kernels for 0%

commit v1 on v0

v1 whole, which is shorter than its diff:
```python
import math

import jax
import jax.numpy as jnp
from jax import lax
from jax.experimental import pallas as pl
from jax.experimental.pallas import tpu as pltpu
from jax.sharding import PartitionSpec as P

BLOCK = 128
ROWS = 768
COLS = 256
GROUP = 48
OWN = 6
HALF = ROWS // 2
MESH = pl.DeviceIdType.MESH

decay_rate = 0.9
outer_rate = 0.7
keep = 1.0 - outer_rate * (1.0 + decay_rate)
root = 1.0 / math.sqrt(BLOCK)


def split3(values):
    high = values.astype(jnp.bfloat16)
    rest = values - high.astype(jnp.float32)
    middle = rest.astype(jnp.bfloat16)
    low = (rest - middle.astype(jnp.float32)).astype(jnp.bfloat16)
    return high, middle, low


def rotate(values, table):
    parts = [jnp.dot(part, table, preferred_element_type=jnp.float32) for part in split3(values)]
    return (parts[0] + parts[1] + parts[2]) * root


def kernel(
    tokens, query_weight, global_params, local_params, momentum, inner_steps, replica_tokens, plan,
    queries, residual, new_momentum,
    token_buf, weight_buf, global_buf, local_buf, momentum_buf, table_buf, term_buf,
    got1, send2, got2, slot_send, slot_got, moment_send, moment_got, send3, got3, gathered,
    load_sem, s1_send, s1_got, s2_send, s2_got, s3_send, s3_got, s4_send, s4_got, s5_send, s5_got,
    w_send, w_got, m_send, m_got,
):
    rep, shard = lax.axis_index("rep"), lax.axis_index("fsdp")
    core = lax.rem(rep, 2)
    z = lax.rem(rep // 2, 32)
    y = rep // 64
    ring = z // 4
    kind = lax.rem(rep, 8)
    group = 8 * y + kind
    twin = 64 * y + 8 * kind + ring
    paired = ring != kind
    x, y_hi = shard // 2, lax.rem(shard, 2)
    sign = 1 - 2 * lax.rem(z, 2)

    def at(dy, dz, dc):
        ny, nz, nc = lax.rem(y + dy, 2), lax.rem(z + dz + 32, 32), lax.rem(core + dc, 2)
        return 64 * ny + 2 * nz + nc, 8 * ny + 2 * lax.rem(nz, 4) + nc

    def around(step):
        return lax.rem(ring + step, 8)

    right, left = 2 * lax.rem(x + 1, 4) + y_hi, 2 * lax.rem(x + 3, 4) + y_hi
    across = 2 * x + 1 - y_hi

    loads = []
    for index, (source, target) in enumerate((
        (local_params.at[0], local_buf), (global_params, global_buf), (momentum, momentum_buf),
        (query_weight.at[0], weight_buf.at[shard]), (tokens, token_buf),
    )):
        loads.append(pltpu.make_async_copy(source, target, load_sem.at[index]))
        loads[-1].start()

    barrier = pltpu.get_barrier_semaphore()
    count = 0
    for dy in (0, 1):
        for dz in (0, 1, -1, 2, -2):
            for dc in (0, 1):
                if (dy, dz, dc) != (0, 0, 0):
                    pl.semaphore_signal(barrier, inc=1, device_id=(at(dy, dz, dc)[0], shard), device_id_type=MESH)
                    count += 1
    for step in range(1, 8):
        pl.semaphore_signal(
            barrier, inc=1, device_id=(64 * y + 8 * around(step) + kind, shard), device_id_type=MESH
        )
        count += 1
    for other in (right, left, across):
        pl.semaphore_signal(barrier, inc=1, device_id=(rep, other), device_id_type=MESH)
        count += 1

    @pl.when(paired)
    def _():
        pl.semaphore_signal(barrier, inc=1, device_id=(twin, shard), device_id_type=MESH)

    row = lax.broadcasted_iota(jnp.int32, (BLOCK, BLOCK), 0)
    col = lax.broadcasted_iota(jnp.int32, (BLOCK, BLOCK), 1)
    bits = row & col
    bits = bits ^ (bits >> 4)
    bits = bits ^ (bits >> 2)
    bits = bits ^ (bits >> 1)
    signs = (1 - 2 * (bits & 1)).astype(jnp.float32).astype(jnp.bfloat16)
    table_buf[...] = jnp.zeros_like(table_buf)
    table_buf[:BLOCK, :BLOCK] = signs
    table_buf[BLOCK:, BLOCK:] = signs

    ratio = replica_tokens[...].astype(jnp.float32) / inner_steps[...].astype(jnp.float32)
    lane = lax.broadcasted_iota(jnp.int32, (1, 128), 1)
    mine = jnp.sum(jnp.where(lane == rep, ratio, 0.0), axis=1, keepdims=True)
    share = mine / jnp.sum(ratio, axis=1, keepdims=True)

    loads[0].wait()
    loads[1].wait()

    def code_rows(step, carry):
        rows = pl.ds(pl.multiple_of(step * 192, 192), 192)
        delta = global_buf[rows, :] - local_buf[rows, :].astype(jnp.float32)
        rotated = rotate(delta, table_buf[...])
        for side in (0, 1):
            block = rotated[:, side * BLOCK:(side + 1) * BLOCK]
            scale = jnp.max(jnp.abs(block), axis=1, keepdims=True) + 1e-06
            code = (block / scale).astype(jnp.bfloat16)
            term = code.astype(jnp.float32) * scale * share
            term_buf[rows, side * BLOCK:(side + 1) * BLOCK] = term.astype(jnp.bfloat16)
        return carry

    lax.fori_loop(0, ROWS // 192, code_rows, 0)

    loads[2].wait()
    slot = momentum_buf[plan[0]]
    slot_send[...] = jnp.concatenate([slot[:, :BLOCK], slot[:, BLOCK:]], axis=0)

    pl.semaphore_wait(barrier, count + jnp.where(paired, 1, 0))

    def remote(source, target, sends, gots, index, device):
        return pltpu.make_async_remote_copy(
            src_ref=source, dst_ref=target, send_sem=sends.at[index], recv_sem=gots.at[index],
            device_id=device, device_id_type=MESH,
        )

    hops = (0, 1, -1, 2 * sign)
    window = [(dy, index, dc) for dy in (1, 0) for index in (3, 1, 2, 0) for dc in (1, 0)][:-1]
    first = []
    for dy, index, dc in window:
        device, rows = at(dy, hops[index], dc)
        place = 8 * dy + 2 * index + dc
        first.append(remote(
            term_buf.at[pl.ds(pl.multiple_of(rows * GROUP, GROUP), GROUP), :], got1.at[place],
            s1_send, s1_got, place, (device, shard),
        ))
        first[-1].start()

    own_weight = query_weight.at[0]
    ring1 = [
        remote(own_weight, weight_buf.at[shard], w_send, w_got, 0, (rep, right)),
        remote(own_weight, weight_buf.at[shard], w_send, w_got, 1, (rep, left)),
    ]
    for copy in ring1:
        copy.start()

    slot_copy = remote(slot_send, slot_got, m_send, m_got, 0, (twin, shard))

    @pl.when(paired)
    def _():
        slot_copy.start()

    @pl.when(jnp.logical_not(paired))
    def _():
        slot_got[...] = slot_send[...]

    loads[3].wait()
    loads[4].wait()

    def product(block):
        depth = pl.ds(pl.multiple_of(block * ROWS, ROWS), ROWS)
        return jnp.dot(token_buf[:, depth], weight_buf[block], preferred_element_type=jnp.float32)

    total = product(shard)

    own_rows = global_buf[pl.ds(pl.multiple_of(group * GROUP, GROUP), GROUP), :]
    own_global = jnp.zeros((OWN, COLS), jnp.float32)
    for index in range(8):
        own_global = own_global + jnp.where(ring == index, own_rows[OWN * index:OWN * (index + 1), :], 0.0)
    own_global = jnp.concatenate([own_global[:, :BLOCK], own_global[:, BLOCK:]], axis=0)

    summed = term_buf[pl.ds(pl.multiple_of(group * GROUP, GROUP), GROUP), :].astype(jnp.float32)
    for (dy, index, dc), copy in reversed(list(zip(window, first))):
        copy.wait_recv()
        summed = summed + got1[8 * dy + 2 * index + dc].astype(jnp.float32)
    for index in range(8):
        send2[index, :OWN, :] = summed[OWN * index:OWN * (index + 1), :BLOCK]
        send2[index, OWN:, :] = summed[OWN * index:OWN * (index + 1), BLOCK:]

    order = (4, 3, 5, 2, 6, 1, 7)
    second = []
    for step in order:
        other = around(step)
        second.append(remote(
            send2.at[other], got2.at[step], s2_send, s2_got, step, (64 * y + 8 * other + kind, shard),
        ))
        second[-1].start()

    across_copy = remote(own_weight, weight_buf.at[shard], w_send, w_got, 4, (rep, across))
    across_copy.start()

    block_left, block_right = left, right

    def forward(block_from_left, block_from_right, base):
        top, bottom = pl.ds(0, HALF), pl.ds(HALF, HALF)
        return [
            remote(weight_buf.at[block_from_left, top, :], weight_buf.at[block_from_left, top, :],
                   w_send, w_got, base, (rep, right)),
            remote(weight_buf.at[block_from_right, bottom, :], weight_buf.at[block_from_right, bottom, :],
                   w_send, w_got, base + 1, (rep, left)),
        ]

    for copy in ring1:
        copy.wait_recv()
    ring2 = forward(block_left, block_right, 2)
    for copy in ring2:
        copy.start()
    total = total + product(left) + product(right)

    @pl.when(paired)
    def _():
        slot_copy.wait_recv()

    owned = send2[ring]
    for step, copy in reversed(list(zip(order, second))):
        copy.wait_recv()
        owned = owned + got2[step]
    average = rotate(owned, table_buf[:BLOCK, :BLOCK])
    moment = decay_rate * slot_got[...] + average
    moment_send[...] = moment
    rest = (1.0 - keep) * own_global - outer_rate * (average + decay_rate * moment)
    send3[:2 * OWN, :] = rest
    send3[2 * OWN:, :] = jnp.zeros((4, BLOCK), jnp.float32)
    got3[ring] = send3[...].astype(jnp.bfloat16)

    third = []
    for step in order:
        other = around(step)
        third.append(remote(
            got3.at[ring], got3.at[ring], s3_send, s3_got, step, (64 * y + 8 * other + kind, shard),
        ))
        third[-1].start()
    moment_copy = remote(moment_send, moment_got, m_send, m_got, 1, (twin, shard))

    @pl.when(paired)
    def _():
        moment_copy.start()

    @pl.when(jnp.logical_not(paired))
    def _():
        moment_got[...] = moment_send[...]

    across_copy.wait_recv()
    ring3 = [
        remote(weight_buf.at[across], weight_buf.at[across], w_send, w_got, 5, (rep, right)),
        remote(weight_buf.at[across], weight_buf.at[across], w_send, w_got, 6, (rep, left)),
    ]
    for copy in ring3:
        copy.start()
    far = 2 * lax.rem(x + 2, 4) + y_hi
    for copy in ring2:
        copy.wait_recv()
    total = total + product(across) + product(far)

    for copy in reversed(third):
        copy.wait_recv()
    pieces = got3[...].astype(jnp.float32)
    whole = jnp.concatenate([
        jnp.concatenate([pieces[index, :OWN, :] for index in range(8)], axis=0),
        jnp.concatenate([pieces[index, OWN:2 * OWN, :] for index in range(8)], axis=0),
    ], axis=1)
    gathered[pl.ds(pl.multiple_of(group * GROUP, GROUP), GROUP), :] = whole.astype(jnp.bfloat16)

    def rows_of(number):
        return gathered.at[pl.ds(pl.multiple_of(number * GROUP, GROUP), GROUP), :]

    near = [(dy, index) for dy in (1, 0) for index in (3, 1, 2, 0)][:-1]
    fourth = []
    for dy, index in near:
        fourth.append(remote(
            rows_of(group), rows_of(group), s4_send, s4_got, 4 * dy + index,
            (at(dy, -hops[index], 0)[0], shard),
        ))
        fourth[-1].start()
    sibling = at(0, 0, 1)[0]
    fifth = [remote(rows_of(group), rows_of(group), s5_send, s5_got, 0, (sibling, shard))]
    fifth[0].start()

    for copy in ring3:
        copy.wait_recv()
    across_left, across_right = 2 * lax.rem(x + 3, 4) + 1 - y_hi, 2 * lax.rem(x + 1, 4) + 1 - y_hi
    ring4 = forward(across_left, across_right, 7)
    for copy in ring4:
        copy.start()
    total = total + product(across_left) + product(across_right)

    @pl.when(paired)
    def _():
        moment_copy.wait_recv()

    new_momentum[...] = jnp.concatenate([moment_got[:OWN, :], moment_got[OWN:, :]], axis=1)

    for (dy, index), copy in reversed(list(zip(near, fourth))):
        copy.wait_recv()
        number = at(dy, hops[index], 0)[1]
        fifth.append(remote(
            rows_of(number), rows_of(number), s5_send, s5_got, 4 * dy + index, (sibling, shard),
        ))
        fifth[-1].start()
    for copy in ring4:
        copy.wait_recv()
    total = total + product(2 * lax.rem(x + 2, 4) + 1 - y_hi)
    queries[...] = total.astype(jnp.bfloat16)
    for copy in fifth:
        copy.wait_recv()
    residual[...] = gathered[...]

    for copy in first + ring1 + second + [across_copy] + ring2 + third + ring3 + fourth + ring4 + fifth:
        copy.wait_send()

    @pl.when(paired)
    def _():
        slot_copy.wait_send()
        moment_copy.wait_send()


def local(
    tokens, query_weight, global_params, local_params, momentum, inner_steps, replica_tokens, plan
):
    anywhere = pl.BlockSpec(memory_space=pl.ANY)
    vmem = pl.BlockSpec(memory_space=pltpu.VMEM)
    smem = pl.BlockSpec(memory_space=pltpu.SMEM)
    dma = pltpu.SemaphoreType.DMA
    f32, bf16 = jnp.float32, jnp.bfloat16
    queries, residual, new_momentum = pl.pallas_call(
        kernel,
        out_shape=(
            jax.ShapeDtypeStruct((224, 128), bf16),
            jax.ShapeDtypeStruct((ROWS, COLS), bf16),
            jax.ShapeDtypeStruct((OWN, COLS), f32),
        ),
        in_specs=[anywhere] * 5 + [vmem, vmem, smem],
        out_specs=(vmem, vmem, vmem),
        scratch_shapes=[
            pltpu.VMEM((224, 6144), bf16),
            pltpu.VMEM((8, ROWS, 128), bf16),
            pltpu.VMEM((ROWS, COLS), f32),
            pltpu.VMEM((ROWS, COLS), bf16),
            pltpu.VMEM((8, OWN, COLS), f32),
            pltpu.VMEM((COLS, COLS), bf16),
            pltpu.VMEM((ROWS, COLS), bf16),
            pltpu.VMEM((16, GROUP, COLS), bf16),
            pltpu.VMEM((8, 2 * OWN, BLOCK), f32),
            pltpu.VMEM((8, 2 * OWN, BLOCK), f32),
            pltpu.VMEM((2 * OWN, BLOCK), f32),
            pltpu.VMEM((2 * OWN, BLOCK), f32),
            pltpu.VMEM((2 * OWN, BLOCK), f32),
            pltpu.VMEM((2 * OWN, BLOCK), f32),
            pltpu.VMEM((16, BLOCK), f32),
            pltpu.VMEM((8, 16, BLOCK), bf16),
            pltpu.VMEM((ROWS, COLS), bf16),
            dma((5,)),
            dma((16,)), dma((16,)),
            dma((8,)), dma((8,)),
            dma((8,)), dma((8,)),
            dma((8,)), dma((8,)),
            dma((8,)), dma((8,)),
            dma((9,)), dma((9,)),
            dma((2,)), dma((2,)),
        ],
        compiler_params=pltpu.CompilerParams(
            collective_id=0, has_side_effects=True, vmem_limit_bytes=32 * 1024 * 1024
        ),
        name="outer_step",
    )(
        tokens, query_weight, global_params, local_params, momentum,
        inner_steps.reshape(1, 128), replica_tokens.reshape(1, 128), plan,
    )
    new_params = keep * global_params + residual.astype(f32)
    return queries, new_params, new_momentum


def solution(mesh):
    return jax.shard_map(
        local,
        mesh=mesh,
        in_specs=(
            P(("rep", "fsdp"), None),
            P("rep", "fsdp", None),
            P("fsdp", None),
            P("rep", "fsdp", None),
            P(None, ("fsdp", "rep"), None),
            P(),
            P(),
            P(),
        ),
        out_specs=(P(("rep", "fsdp"), None), P("fsdp", None), P(("fsdp", "rep"), None)),
        check_vma=False,
    )
```

time: 848 us -> 78.6 us (0.09)
  waiting for transfers between devices: 675 us -> 0 us
  blocking collectives: 138 us -> 0 us
  Pallas kernels: 0 us -> 67.7 us
  between operations: 17.5 us -> 1.3 us
    psum x1 -> x0, waiting for transfers between devices: 674 us -> none  [local(): summed = lax.psum(term, 'rep')]
    all_gather x1 -> x0, blocking collectives: 138 us -> none  [local(): slot_full = lax.all_gather(slot, 'rep', axis=0, tiled=True)]
    pallas_call x0 -> x1, Pallas kernels: none -> 67.7 us  [local(): pl.pallas_call(kernel, out_shape=(jax.ShapeDtypeStruct((224, 128), bf16),...]
  transfers between devices with their start and end apart: 2 -> 0, of which waited for: 1 -> 0; matrix products, arithmetic and copies ran while one was open for 1% -> 0% of each run, Pallas kernels for 0% -> 0%
where the time goes in v1:
time: 78.6 us; the launch traced here: 78.2 us
  Pallas kernels  67.7 us (86%)
  local copies, waits for them, and re-layouts  8.17 us (10%)
  between operations  1.3 us (2%)
  other arithmetic  0.97 us (1%)
    pallas_call x1, Pallas kernels, local(): pl.pallas_call(kernel, out_shape=(jax.ShapeDtypeStruct((224, 128), bf16),...  67.7 us
    unnamed x15, local copies, waits for them, and re-layouts  8.17 us

profile of v1, /device:TPU:1, one launch (start us, length us, event | category | flops | bytes accessed | tf_op | source)
XLA Modules:
  0.0 78.2 jit_solution(16783910003628406181)
XLA Ops:
  1.3 0.8 %copy.11.momentum = f32[8,6,256]{2,1,0:T(8,128)S(1)} copy(f32[8,6,256]{2,0,1:T(8,128)} %param.12) | data formatting | bytes 98304 | tf_op args[4]
  2.1 0.0 copy-start
  2.1 1.1 %copy-done = f32[768,256]{1,0:T(8,128)S(1)} copy-done((f32[768,256]{1,0:T(8,128)S(1)}, f32[768,256]{1,0:T(8,128)}, u32[]{:S(2)}) %copy-start) | copy-done | bytes 786456
  3.2 0.0 copy-start.1
  3.2 1.8 %copy-done.1 = bf16[224,6144]{1,0:T(8,128)(2,1)S(1)} copy-done((bf16[224,6144]{1,0:T(8,128)(2,1)S(1)}, bf16[224,6144]{1,0:T(8,128)(2,1)}, u32[]{:S(2)}) %copy-start.1) | copy-done | bytes 2752536
  5.0 0.0 copy-start.2
  5.0 1.0 %copy-done.2 = bf16[1,768,256]{2,1,0:T(8,128)(2,1)S(1)} copy-done((bf16[1,768,256]{2,1,0:T(8,128)(2,1)S(1)}, bf16[1,768,256]{2,1,0:T(8,128)(2,1)}, u32[]{:S(2)}) %copy-start.2) | copy-done | bytes 393240
  6.0 0.0 copy-start.3
  6.0 0.9 %copy-done.3 = bf16[1,768,128]{2,1,0:T(8,128)(2,1)S(1)} copy-done((bf16[1,768,128]{2,1,0:T(8,128)(2,1)S(1)}, bf16[1,768,128]{2,1,0:T(8,128)(2,1)}, u32[]{:S(2)}) %copy-start.3) | copy-done | bytes 196632
  6.9 0.0 copy-start.4
  6.9 0.7 copy-done.4
  7.6 0.0 copy-start.5
  7.6 0.7 copy-done.5
  8.2 67.7 %outer_step.1 = (bf16[224,128]{1,0:T(8,128)(2,1)S(1)}, bf16[768,256]{1,0:T(8,128)(2,1)S(1)}, f32[6,256]{1,0:T(8,128)S(1)}) custom-call(bf16[224,6144]{1,0:T(8,128)(2,1)S(1)} %copy-done.1, bf16[1,768,128]{2,1,0:T(8,128)(2,1)S(1)} %copy-done.3, f32[768,256]{1,0:T(8,128)S(1)} %copy-done, bf16[1,768,256]{2,1,0:T(8,128)(2,1)S(1)} %copy-done.2, ...), custom_call_target="tpu_custom_call" | custom-call | tf_op jit(solution)/shard_map/outer_step/pallas_call | solution.py:339
  76.0 1.0 %convert_add_fusion = f32[768,256]{1,0:T(8,128)} fusion(bf16[768,256]{1,0:T(8,128)(2,1)S(1)} %get-tuple-element.7, f32[768,256]{1,0:T(8,128)S(1)} %copy-done), kind=kLoop, calls=%fused_computation | loop fusion | flops 589824 | bytes 1966080 | tf_op jit(solution)/shard_map/add | solution.py:383
  76.9 0.6 copy.15
  77.6 0.6 copy.16
Async XLA Ops:
  2.1 1.1 %copy-start = (f32[768,256]{1,0:T(8,128)S(1)}, f32[768,256]{1,0:T(8,128)}, u32[]{:S(2)}) copy-start(f32[768,256]{1,0:T(8,128)} %global_params.1) | copy-start | bytes 2359300
  3.2 1.8 %copy-start.1 = (bf16[224,6144]{1,0:T(8,128)(2,1)S(1)}, bf16[224,6144]{1,0:T(8,128)(2,1)}, u32[]{:S(2)}) copy-start(bf16[224,6144]{1,0:T(8,128)(2,1)} %tokens.1) | copy-start | bytes 8257540
  5.0 1.0 %copy-start.2 = (bf16[1,768,256]{2,1,0:T(8,128)(2,1)S(1)}, bf16[1,768,256]{2,1,0:T(8,128)(2,1)}, u32[]{:S(2)}) copy-start(bf16[1,768,256]{2,1,0:T(8,128)(2,1)} %local_params.1) | copy-start | bytes 1179652
  6.0 0.9 %copy-start.3 = (bf16[1,768,128]{2,1,0:T(8,128)(2,1)S(1)}, bf16[1,768,128]{2,1,0:T(8,128)(2,1)}, u32[]{:S(2)}) copy-start(bf16[1,768,128]{2,1,0:T(8,128)(2,1)} %query_weight.1) | copy-start | bytes 589828
  6.9 0.7 copy-start.4
  7.6 0.7 copy-start.5

commit v2 on v1

--- a/solution.py
+++ b/solution.py
@@ -18,6 +18,7 @@
 decay_rate = 0.9
 outer_rate = 0.7
 keep = 1.0 - outer_rate * (1.0 + decay_rate)
+slot_share = decay_rate * decay_rate / (1.0 + decay_rate)
 root = 1.0 / math.sqrt(BLOCK)
 
 
@@ -38,9 +39,9 @@
     tokens, query_weight, global_params, local_params, momentum, inner_steps, replica_tokens, plan,
     queries, residual, new_momentum,
     token_buf, weight_buf, global_buf, local_buf, momentum_buf, table_buf, term_buf,
-    got1, send2, got2, slot_send, slot_got, moment_send, moment_got, send3, got3, gathered,
+    got1, send2, got2, moment_send, moment_got, send3, got3, gathered,
     load_sem, s1_send, s1_got, s2_send, s2_got, s3_send, s3_got, s4_send, s4_got, s5_send, s5_got,
-    w_send, w_got, m_send, m_got,
+    w_send, w_got, m_send, m_got, far_sem,
 ):
     rep, shard = lax.axis_index("rep"), lax.axis_index("fsdp")
     core = lax.rem(rep, 2)
@@ -51,6 +52,7 @@
     group = 8 * y + kind
     twin = 64 * y + 8 * kind + ring
     paired = ring != kind
+    chunk = 8 * y + ring
     x, y_hi = shard // 2, lax.rem(shard, 2)
     sign = 1 - 2 * lax.rem(z, 2)
 
@@ -80,18 +82,12 @@
                 if (dy, dz, dc) != (0, 0, 0):
                     pl.semaphore_signal(barrier, inc=1, device_id=(at(dy, dz, dc)[0], shard), device_id_type=MESH)
                     count += 1
-    for step in range(1, 8):
-        pl.semaphore_signal(
-            barrier, inc=1, device_id=(64 * y + 8 * around(step) + kind, shard), device_id_type=MESH
-        )
+    for dz in (4, -4, 8, -8):
+        pl.semaphore_signal(barrier, inc=1, device_id=(at(0, dz, 0)[0], shard), device_id_type=MESH)
         count += 1
     for other in (right, left, across):
         pl.semaphore_signal(barrier, inc=1, device_id=(rep, other), device_id_type=MESH)
         count += 1
-
-    @pl.when(paired)
-    def _():
-        pl.semaphore_signal(barrier, inc=1, device_id=(twin, shard), device_id_type=MESH)
 
     row = lax.broadcasted_iota(jnp.int32, (BLOCK, BLOCK), 0)
     col = lax.broadcasted_iota(jnp.int32, (BLOCK, BLOCK), 1)
@@ -127,10 +123,16 @@
     lax.fori_loop(0, ROWS // 192, code_rows, 0)
 
     loads[2].wait()
-    slot = momentum_buf[plan[0]]
-    slot_send[...] = jnp.concatenate([slot[:, :BLOCK], slot[:, BLOCK:]], axis=0)
-
-    pl.semaphore_wait(barrier, count + jnp.where(paired, 1, 0))
+    fragment = lax.broadcasted_iota(jnp.int32, momentum_buf.shape, 1)
+    slot = jnp.sum(jnp.where(fragment == plan[0], momentum_buf[...], 0.0), axis=1)
+    spread = jnp.concatenate([jnp.where(kind == index, slot, 0.0) for index in range(8)], axis=0)
+    chunk_rows = pl.ds(pl.multiple_of(chunk * GROUP, GROUP), GROUP)
+    shifted = term_buf[chunk_rows, :].astype(jnp.float32) + slot_share * rotate(spread, table_buf[...])
+    term_buf[chunk_rows, :] = shifted.astype(jnp.bfloat16)
+
+    pl.semaphore_wait(barrier, count)
+    for dz in (8, -8):
+        pl.semaphore_signal(far_sem, inc=1, device_id=(at(0, dz, 0)[0], shard), device_id_type=MESH)
 
     def remote(source, target, sends, gots, index, device):
         return pltpu.make_async_remote_copy(
@@ -158,16 +160,6 @@
     for copy in ring1:
         copy.start()
 
-    slot_copy = remote(slot_send, slot_got, m_send, m_got, 0, (twin, shard))
-
-    @pl.when(paired)
-    def _():
-        slot_copy.start()
-
-    @pl.when(jnp.logical_not(paired))
-    def _():
-        slot_got[...] = slot_send[...]
-
     loads[3].wait()
     loads[4].wait()
 
@@ -192,6 +184,7 @@
         send2[index, OWN:, :] = summed[OWN * index:OWN * (index + 1), BLOCK:]
 
     order = (4, 3, 5, 2, 6, 1, 7)
+    pl.semaphore_wait(far_sem, 2)
     second = []
     for step in order:
         other = around(step)
@@ -221,18 +214,13 @@
         copy.start()
     total = total + product(left) + product(right)
 
-    @pl.when(paired)
-    def _():
-        slot_copy.wait_recv()
-
     owned = send2[ring]
     for step, copy in reversed(list(zip(order, second))):
         copy.wait_recv()
         owned = owned + got2[step]
     average = rotate(owned, table_buf[:BLOCK, :BLOCK])
-    moment = decay_rate * slot_got[...] + average
-    moment_send[...] = moment
-    rest = (1.0 - keep) * own_global - outer_rate * (average + decay_rate * moment)
+    moment_send[...] = average
+    rest = (1.0 - keep) * (own_global - average)
     send3[:2 * OWN, :] = rest
     send3[2 * OWN:, :] = jnp.zeros((4, BLOCK), jnp.float32)
     got3[ring] = send3[...].astype(jnp.bfloat16)
@@ -244,7 +232,7 @@
             got3.at[ring], got3.at[ring], s3_send, s3_got, step, (64 * y + 8 * other + kind, shard),
         ))
         third[-1].start()
-    moment_copy = remote(moment_send, moment_got, m_send, m_got, 1, (twin, shard))
+    moment_copy = remote(moment_send, moment_got, m_send, m_got, 0, (twin, shard))
 
     @pl.when(paired)
     def _():
@@ -302,7 +290,8 @@
     def _():
         moment_copy.wait_recv()
 
-    new_momentum[...] = jnp.concatenate([moment_got[:OWN, :], moment_got[OWN:, :]], axis=1)
+    shifted_rows = jnp.concatenate([moment_got[:OWN, :], moment_got[OWN:, :]], axis=1)
+    new_momentum[...] = shifted_rows + (decay_rate - slot_share) * slot
 
     for (dy, index), copy in reversed(list(zip(near, fourth))):
         copy.wait_recv()
@@ -324,7 +313,6 @@
 
     @pl.when(paired)
     def _():
-        slot_copy.wait_send()
         moment_copy.wait_send()
 
 
@@ -350,14 +338,12 @@
             pltpu.VMEM((8, ROWS, 128), bf16),
             pltpu.VMEM((ROWS, COLS), f32),
             pltpu.VMEM((ROWS, COLS), bf16),
-            pltpu.VMEM((8, OWN, COLS), f32),
+            pltpu.VMEM((OWN, 8, COLS), f32),
             pltpu.VMEM((COLS, COLS), bf16),
             pltpu.VMEM((ROWS, COLS), bf16),
             pltpu.VMEM((16, GROUP, COLS), bf16),
             pltpu.VMEM((8, 2 * OWN, BLOCK), f32),
             pltpu.VMEM((8, 2 * OWN, BLOCK), f32),
-            pltpu.VMEM((2 * OWN, BLOCK), f32),
-            pltpu.VMEM((2 * OWN, BLOCK), f32),
             pltpu.VMEM((2 * OWN, BLOCK), f32),
             pltpu.VMEM((2 * OWN, BLOCK), f32),
             pltpu.VMEM((16, BLOCK), f32),
@@ -370,14 +356,15 @@
             dma((8,)), dma((8,)),
             dma((8,)), dma((8,)),
             dma((9,)), dma((9,)),
-            dma((2,)), dma((2,)),
+            dma((1,)), dma((1,)),
+            pltpu.SemaphoreType.REGULAR,
         ],
         compiler_params=pltpu.CompilerParams(
-            collective_id=0, has_side_effects=True, vmem_limit_bytes=32 * 1024 * 1024
+            collective_id=0, has_side_effects=True, vmem_limit_bytes=60 * 1024 * 1024
         ),
         name="outer_step",
     )(
-        tokens, query_weight, global_params, local_params, momentum,
+        tokens, query_weight, global_params, local_params, momentum.transpose(1, 0, 2),
         inner_steps.reshape(1, 128), replica_tokens.reshape(1, 128), plan,
     )
     new_params = keep * global_params + residual.astype(f32)

time: 78.6 us -> 68.2 us (0.87)
  Pallas kernels: 67.7 us -> 61.9 us
  local copies, waits for them, and re-layouts: 8.17 us -> 2.74 us
  other arithmetic: 0.97 us -> 1.98 us
    pallas_call x1, Pallas kernels: 67.7 us -> 61.9 us  [local(): pl.pallas_call(kernel, out_shape=(jax.ShapeDtypeStruct((224, 128), bf16),...]
    unnamed x15 -> x4, local copies, waits for them, and re-layouts: 8.17 us -> 2.74 us
    add x1, other arithmetic: 0.97 us -> 1.98 us  [local(): new_params = keep * global_params + residual.astype(f32)]
where the time goes in v2:
time: 68.2 us; the launch traced here: 68 us
  Pallas kernels  61.9 us (91%)
  local copies, waits for them, and re-layouts  2.74 us (4%)
  other arithmetic  1.98 us (3%)
  between operations  1.38 us (2%)
    pallas_call x1, Pallas kernels, local(): pl.pallas_call(kernel, out_shape=(jax.ShapeDtypeStruct((224, 128), bf16),...  61.9 us
    unnamed x4, local copies, waits for them, and re-layouts  2.74 us
    add x1, other arithmetic, local(): new_params = keep * global_params + residual.astype(f32)  1.98 us

profile of v2, /device:TPU:1, one launch (start us, length us, event | category | flops | bytes accessed | tf_op | source)
XLA Modules:
  0.0 68.0 jit_solution(15661227407682757390)
XLA Ops:
  0.6 0.0 copy-start
  1.4 61.9 %outer_step.1 = (bf16[224,128]{1,0:T(8,128)(2,1)}, bf16[768,256]{1,0:T(8,128)(2,1)}, f32[6,256]{1,0:T(8,128)}) custom-call(bf16[224,6144]{1,0:T(8,128)(2,1)} %tokens.1, bf16[1,768,128]{2,1,0:T(8,128)(2,1)} %query_weight.1, f32[768,256]{1,0:T(8,128)} %global_params.1, bf16[1,768,256]{2,1,0:T(8,128)(2,1)} %local_params.1, f32[6,8,256]{2,1,0:T(8,128)} %bitcast.3, ...), custom_call_target="tpu_custom_call" | custom-call | tf_op jit(solution)/shard_map/outer_step/pallas_call | solution.py:327
  63.2 0.0 copy-done
  63.2 2.0 %convert_add_fusion = f32[768,256]{1,0:T(8,128)} fusion(bf16[768,256]{1,0:T(8,128)(2,1)} %get-tuple-element.7, f32[768,256]{1,0:T(8,128)S(1)} %copy-done), kind=kLoop, calls=%fused_computation | loop fusion | flops 589824 | bytes 1966080 | tf_op jit(solution)/shard_map/add | solution.py:370
  65.2 1.4 %copy.14 = bf16[224,128]{1,0:T(8,128)(2,1)} copy(bf16[224,128]{1,0:T(8,128)(2,1)} %get-tuple-element.12) | data formatting | bytes 114688
  66.7 1.3 %copy.15 = f32[6,256]{1,0:T(8,128)} copy(f32[6,256]{1,0:T(8,128)} %get-tuple-element.14) | data formatting | bytes 12288
Async XLA Ops:
  0.6 62.6 %copy-start = (f32[768,256]{1,0:T(8,128)S(1)}, f32[768,256]{1,0:T(8,128)}, u32[]{:S(2)}) copy-start(f32[768,256]{1,0:T(8,128)} %global_params.1) | copy-start | bytes 2359300

commit v3 on v2

--- a/solution.py
+++ b/solution.py
@@ -38,10 +38,10 @@
 def kernel(
     tokens, query_weight, global_params, local_params, momentum, inner_steps, replica_tokens, plan,
     queries, residual, new_momentum,
-    token_buf, weight_buf, global_buf, local_buf, momentum_buf, table_buf, term_buf,
-    got1, send2, got2, moment_send, moment_got, send3, got3, gathered,
+    token_buf, weight_buf, global_buf, local_buf, momentum_buf, table_buf, term_buf, steps_buf, trained_buf,
+    got1, far_send, far_got, moment_send, moment_got, gathered,
     load_sem, s1_send, s1_got, s2_send, s2_got, s3_send, s3_got, s4_send, s4_got, s5_send, s5_got,
-    w_send, w_got, m_send, m_got, far_sem,
+    w_send, w_got, m_send, m_got,
 ):
     rep, shard = lax.axis_index("rep"), lax.axis_index("fsdp")
     core = lax.rem(rep, 2)
@@ -50,8 +50,7 @@
     ring = z // 4
     kind = lax.rem(rep, 8)
     group = 8 * y + kind
-    twin = 64 * y + 8 * kind + ring
-    paired = ring != kind
+    hub = ring == 0
     chunk = 8 * y + ring
     x, y_hi = shard // 2, lax.rem(shard, 2)
     sign = 1 - 2 * lax.rem(z, 2)
@@ -59,9 +58,6 @@
     def at(dy, dz, dc):
         ny, nz, nc = lax.rem(y + dy, 2), lax.rem(z + dz + 32, 32), lax.rem(core + dc, 2)
         return 64 * ny + 2 * nz + nc, 8 * ny + 2 * lax.rem(nz, 4) + nc
-
-    def around(step):
-        return lax.rem(ring + step, 8)
 
     right, left = 2 * lax.rem(x + 1, 4) + y_hi, 2 * lax.rem(x + 3, 4) + y_hi
     across = 2 * x + 1 - y_hi
@@ -70,6 +66,7 @@
     for index, (source, target) in enumerate((
         (local_params.at[0], local_buf), (global_params, global_buf), (momentum, momentum_buf),
         (query_weight.at[0], weight_buf.at[shard]), (tokens, token_buf),
+        (inner_steps, steps_buf), (replica_tokens, trained_buf),
     )):
         loads.append(pltpu.make_async_copy(source, target, load_sem.at[index]))
         loads[-1].start()
@@ -82,12 +79,14 @@
                 if (dy, dz, dc) != (0, 0, 0):
                     pl.semaphore_signal(barrier, inc=1, device_id=(at(dy, dz, dc)[0], shard), device_id_type=MESH)
                     count += 1
-    for dz in (4, -4, 8, -8):
-        pl.semaphore_signal(barrier, inc=1, device_id=(at(0, dz, 0)[0], shard), device_id_type=MESH)
-        count += 1
     for other in (right, left, across):
         pl.semaphore_signal(barrier, inc=1, device_id=(rep, other), device_id_type=MESH)
         count += 1
+
+    @pl.when(hub)
+    def _():
+        for step in range(1, 8):
+            pl.semaphore_signal(barrier, inc=1, device_id=(64 * y + 8 * step + kind, shard), device_id_type=MESH)
 
     row = lax.broadcasted_iota(jnp.int32, (BLOCK, BLOCK), 0)
     col = lax.broadcasted_iota(jnp.int32, (BLOCK, BLOCK), 1)
@@ -100,7 +99,9 @@
     table_buf[:BLOCK, :BLOCK] = signs
     table_buf[BLOCK:, BLOCK:] = signs
 
-    ratio = replica_tokens[...].astype(jnp.float32) / inner_steps[...].astype(jnp.float32)
+    loads[5].wait()
+    loads[6].wait()
+    ratio = trained_buf[...].astype(jnp.float32) / steps_buf[...].astype(jnp.float32)
     lane = lax.broadcasted_iota(jnp.int32, (1, 128), 1)
     mine = jnp.sum(jnp.where(lane == rep, ratio, 0.0), axis=1, keepdims=True)
     share = mine / jnp.sum(ratio, axis=1, keepdims=True)
@@ -130,9 +131,7 @@
     shifted = term_buf[chunk_rows, :].astype(jnp.float32) + slot_share * rotate(spread, table_buf[...])
     term_buf[chunk_rows, :] = shifted.astype(jnp.bfloat16)
 
-    pl.semaphore_wait(barrier, count)
-    for dz in (8, -8):
-        pl.semaphore_signal(far_sem, inc=1, device_id=(at(0, dz, 0)[0], shard), device_id_type=MESH)
+    pl.semaphore_wait(barrier, count + jnp.where(hub, 0, 1))
 
     def remote(source, target, sends, gots, index, device):
         return pltpu.make_async_remote_copy(
@@ -169,29 +168,18 @@
 
     total = product(shard)
 
-    own_rows = global_buf[pl.ds(pl.multiple_of(group * GROUP, GROUP), GROUP), :]
-    own_global = jnp.zeros((OWN, COLS), jnp.float32)
-    for index in range(8):
-        own_global = own_global + jnp.where(ring == index, own_rows[OWN * index:OWN * (index + 1), :], 0.0)
-    own_global = jnp.concatenate([own_global[:, :BLOCK], own_global[:, BLOCK:]], axis=0)
-
     summed = term_buf[pl.ds(pl.multiple_of(group * GROUP, GROUP), GROUP), :].astype(jnp.float32)
     for (dy, index, dc), copy in reversed(list(zip(window, first))):
         copy.wait_recv()
         summed = summed + got1[8 * dy + 2 * index + dc].astype(jnp.float32)
-    for index in range(8):
-        send2[index, :OWN, :] = summed[OWN * index:OWN * (index + 1), :BLOCK]
-        send2[index, OWN:, :] = summed[OWN * index:OWN * (index + 1), BLOCK:]
-
-    order = (4, 3, 5, 2, 6, 1, 7)
-    pl.semaphore_wait(far_sem, 2)
-    second = []
-    for step in order:
-        other = around(step)
-        second.append(remote(
-            send2.at[other], got2.at[step], s2_send, s2_got, step, (64 * y + 8 * other + kind, shard),
-        ))
-        second[-1].start()
+    far_send[...] = summed
+
+    def to_hub(index):
+        return remote(far_send, far_got.at[index], s2_send, s2_got, index, (64 * y + kind, shard))
+
+    @pl.when(jnp.logical_not(hub))
+    def _():
+        to_hub(ring).start()
 
     across_copy = remote(own_weight, weight_buf.at[shard], w_send, w_got, 4, (rep, across))
     across_copy.start()
@@ -213,34 +201,6 @@
     for copy in ring2:
         copy.start()
     total = total + product(left) + product(right)
-
-    owned = send2[ring]
-    for step, copy in reversed(list(zip(order, second))):
-        copy.wait_recv()
-        owned = owned + got2[step]
-    average = rotate(owned, table_buf[:BLOCK, :BLOCK])
-    moment_send[...] = average
-    rest = (1.0 - keep) * (own_global - average)
-    send3[:2 * OWN, :] = rest
-    send3[2 * OWN:, :] = jnp.zeros((4, BLOCK), jnp.float32)
-    got3[ring] = send3[...].astype(jnp.bfloat16)
-
-    third = []
-    for step in order:
-        other = around(step)
-        third.append(remote(
-            got3.at[ring], got3.at[ring], s3_send, s3_got, step, (64 * y + 8 * other + kind, shard),
-        ))
-        third[-1].start()
-    moment_copy = remote(moment_send, moment_got, m_send, m_got, 0, (twin, shard))
-
-    @pl.when(paired)
-    def _():
-        moment_copy.start()
-
-    @pl.when(jnp.logical_not(paired))
-    def _():
-        moment_got[...] = moment_send[...]
 
     across_copy.wait_recv()
     ring3 = [
@@ -254,29 +214,63 @@
         copy.wait_recv()
     total = total + product(across) + product(far)
 
-    for copy in reversed(third):
-        copy.wait_recv()
-    pieces = got3[...].astype(jnp.float32)
-    whole = jnp.concatenate([
-        jnp.concatenate([pieces[index, :OWN, :] for index in range(8)], axis=0),
-        jnp.concatenate([pieces[index, OWN:2 * OWN, :] for index in range(8)], axis=0),
-    ], axis=1)
-    gathered[pl.ds(pl.multiple_of(group * GROUP, GROUP), GROUP), :] = whole.astype(jnp.bfloat16)
-
     def rows_of(number):
         return gathered.at[pl.ds(pl.multiple_of(number * GROUP, GROUP), GROUP), :]
 
-    near = [(dy, index) for dy in (1, 0) for index in (3, 1, 2, 0)][:-1]
+    def to_ring(index):
+        return remote(rows_of(group), rows_of(group), s3_send, s3_got, index, (64 * y + 8 * index + kind, shard))
+
+    @pl.when(hub)
+    def _():
+        summed = far_send[...]
+        for index in (1, 2, 3, 7, 6, 5, 4):
+            to_hub(index).wait_recv()
+            summed = summed + far_got[index]
+        average = rotate(summed, table_buf[...])
+        for index in range(8):
+            moment_send[index] = average[OWN * index:OWN * (index + 1), :]
+        own_global = global_buf[pl.ds(pl.multiple_of(group * GROUP, GROUP), GROUP), :]
+        rest = (1.0 - keep) * (own_global - average)
+        gathered[pl.ds(pl.multiple_of(group * GROUP, GROUP), GROUP), :] = rest.astype(jnp.bfloat16)
+        to_ring(1).start()
+
+    @pl.when(jnp.logical_not(hub))
+    def _():
+        to_ring(ring).wait_recv()
+
+    spot = lax.rem(z, 4)
+    near = [(dy, step) for dy in (1, 0) for step in (2, 1, 3, 0)][:-1]
     fourth = []
-    for dy, index in near:
-        fourth.append(remote(
-            rows_of(group), rows_of(group), s4_send, s4_got, 4 * dy + index,
-            (at(dy, -hops[index], 0)[0], shard),
-        ))
+    for dy, step in near:
+        device = 64 * lax.rem(y + dy, 2) + 2 * (4 * ring + lax.rem(spot + step, 4)) + core
+        fourth.append(remote(rows_of(group), rows_of(group), s4_send, s4_got, 4 * dy + step, (device, shard)))
         fourth[-1].start()
     sibling = at(0, 0, 1)[0]
     fifth = [remote(rows_of(group), rows_of(group), s5_send, s5_got, 0, (sibling, shard))]
     fifth[0].start()
+
+    def to_owner(index):
+        return pltpu.make_async_remote_copy(
+            src_ref=moment_send.at[index], dst_ref=moment_got, send_sem=m_send.at[index], recv_sem=m_got,
+            device_id=(8 * group + index, shard), device_id_type=MESH,
+        )
+
+    owner = rep != 64 * y
+
+    @pl.when(hub)
+    def _():
+        for index in (2, 3, 7, 4, 5, 6):
+            to_ring(index).start()
+        for index in range(1, 8):
+            to_owner(index).start()
+
+        @pl.when(owner)
+        def _():
+            to_owner(0).start()
+
+        @pl.when(jnp.logical_not(owner))
+        def _():
+            moment_got[...] = moment_send[0]
 
     for copy in ring3:
         copy.wait_recv()
@@ -286,18 +280,11 @@
         copy.start()
     total = total + product(across_left) + product(across_right)
 
-    @pl.when(paired)
-    def _():
-        moment_copy.wait_recv()
-
-    shifted_rows = jnp.concatenate([moment_got[:OWN, :], moment_got[OWN:, :]], axis=1)
-    new_momentum[...] = shifted_rows + (decay_rate - slot_share) * slot
-
-    for (dy, index), copy in reversed(list(zip(near, fourth))):
-        copy.wait_recv()
-        number = at(dy, hops[index], 0)[1]
+    for (dy, step), copy in reversed(list(zip(near, fourth))):
+        copy.wait_recv()
+        number = 8 * lax.rem(y + dy, 2) + 2 * lax.rem(spot - step + 4, 4) + core
         fifth.append(remote(
-            rows_of(number), rows_of(number), s5_send, s5_got, 4 * dy + index, (sibling, shard),
+            rows_of(number), rows_of(number), s5_send, s5_got, 4 * dy + step, (sibling, shard),
         ))
         fifth[-1].start()
     for copy in ring4:
@@ -308,18 +295,34 @@
         copy.wait_recv()
     residual[...] = gathered[...]
 
-    for copy in first + ring1 + second + [across_copy] + ring2 + third + ring3 + fourth + ring4 + fifth:
+    @pl.when(owner)
+    def _():
+        to_owner(0).wait_recv()
+
+    new_momentum[...] = moment_got[...] + (decay_rate - slot_share) * slot
+
+    for copy in first + ring1 + [across_copy] + ring2 + ring3 + fourth + ring4 + fifth:
         copy.wait_send()
 
-    @pl.when(paired)
-    def _():
-        moment_copy.wait_send()
+    @pl.when(jnp.logical_not(hub))
+    def _():
+        to_hub(ring).wait_send()
+
+    @pl.when(hub)
+    def _():
+        for index in range(1, 8):
+            to_ring(index).wait_send()
+            to_owner(index).wait_send()
+
+        @pl.when(owner)
+        def _():
+            to_owner(0).wait_send()
 
 
 def local(
     tokens, query_weight, global_params, local_params, momentum, inner_steps, replica_tokens, plan
 ):
-    anywhere = pl.BlockSpec(memory_space=pl.ANY)
+    hbm = pl.BlockSpec(memory_space=pl.ANY)
     vmem = pl.BlockSpec(memory_space=pltpu.VMEM)
     smem = pl.BlockSpec(memory_space=pltpu.SMEM)
     dma = pltpu.SemaphoreType.DMA
@@ -331,7 +334,7 @@
             jax.ShapeDtypeStruct((ROWS, COLS), bf16),
             jax.ShapeDtypeStruct((OWN, COLS), f32),
         ),
-        in_specs=[anywhere] * 5 + [vmem, vmem, smem],
+        in_specs=[hbm] * 7 + [smem],
         out_specs=(vmem, vmem, vmem),
         scratch_shapes=[
             pltpu.VMEM((224, 6144), bf16),
@@ -341,23 +344,22 @@
             pltpu.VMEM((OWN, 8, COLS), f32),
             pltpu.VMEM((COLS, COLS), bf16),
             pltpu.VMEM((ROWS, COLS), bf16),
+            pltpu.VMEM((1, 128), jnp.int32),
+            pltpu.VMEM((1, 128), jnp.int32),
             pltpu.VMEM((16, GROUP, COLS), bf16),
-            pltpu.VMEM((8, 2 * OWN, BLOCK), f32),
-            pltpu.VMEM((8, 2 * OWN, BLOCK), f32),
-            pltpu.VMEM((2 * OWN, BLOCK), f32),
-            pltpu.VMEM((2 * OWN, BLOCK), f32),
-            pltpu.VMEM((16, BLOCK), f32),
-            pltpu.VMEM((8, 16, BLOCK), bf16),
+            pltpu.VMEM((GROUP, COLS), f32),
+            pltpu.VMEM((8, GROUP, COLS), f32),
+            pltpu.VMEM((8, OWN, COLS), f32),
+            pltpu.VMEM((OWN, COLS), f32),
             pltpu.VMEM((ROWS, COLS), bf16),
-            dma((5,)),
+            dma((7,)),
             dma((16,)), dma((16,)),
             dma((8,)), dma((8,)),
             dma((8,)), dma((8,)),
             dma((8,)), dma((8,)),
             dma((8,)), dma((8,)),
             dma((9,)), dma((9,)),
-            dma((1,)), dma((1,)),
-            pltpu.SemaphoreType.REGULAR,
+            dma((8,)), dma(()),
         ],
         compiler_params=pltpu.CompilerParams(
             collective_id=0, has_side_effects=True, vmem_limit_bytes=60 * 1024 * 1024

time: 68.2 us -> 65.1 us (0.955)
  the two profiles are of different devices: /device:TPU:1 before, /device:TPU:257 now
where the time goes in v3:
time: 65.1 us; the launch traced here: 64.8 us
  Pallas kernels  58.7 us (90%)
  local copies, waits for them, and re-layouts  2.74 us (4%)
  other arithmetic  1.98 us (3%)
  between operations  1.38 us (2%)
    pallas_call x1, Pallas kernels, local(): pl.pallas_call(kernel, out_shape=(jax.ShapeDtypeStruct((224, 128), bf16),...  58.7 us
    unnamed x4, local copies, waits for them, and re-layouts  2.74 us
    add x1, other arithmetic, local(): new_params = keep * global_params + residual.astype(f32)  1.98 us

profile of v3, /device:TPU:257, one launch (start us, length us, event | category | flops | bytes accessed | tf_op | source)
XLA Modules:
  0.0 64.8 jit_solution(7493003129109804526)
XLA Ops:
  0.6 0.0 copy-start
  1.4 58.7 %outer_step.1 = (bf16[224,128]{1,0:T(8,128)(2,1)}, bf16[768,256]{1,0:T(8,128)(2,1)}, f32[6,256]{1,0:T(8,128)}) custom-call(bf16[224,6144]{1,0:T(8,128)(2,1)} %tokens.1, bf16[1,768,128]{2,1,0:T(8,128)(2,1)} %query_weight.1, f32[768,256]{1,0:T(8,128)} %global_params.1, bf16[1,768,256]{2,1,0:T(8,128)(2,1)} %local_params.1, f32[6,8,256]{2,1,0:T(8,128)} %bitcast.3, ...), custom_call_target="tpu_custom_call" | custom-call | tf_op jit(solution)/shard_map/outer_step/pallas_call | solution.py:330
  60.1 0.0 copy-done
  60.1 2.0 %convert_add_fusion = f32[768,256]{1,0:T(8,128)} fusion(bf16[768,256]{1,0:T(8,128)(2,1)} %get-tuple-element.7, f32[768,256]{1,0:T(8,128)S(1)} %copy-done), kind=kLoop, calls=%fused_computation | loop fusion | flops 589824 | bytes 1966080 | tf_op jit(solution)/shard_map/add | solution.py:372
  62.1 1.4 %copy.14 = bf16[224,128]{1,0:T(8,128)(2,1)} copy(bf16[224,128]{1,0:T(8,128)(2,1)} %get-tuple-element.12) | data formatting | bytes 114688
  63.5 1.3 %copy.15 = f32[6,256]{1,0:T(8,128)} copy(f32[6,256]{1,0:T(8,128)} %get-tuple-element.14) | data formatting | bytes 12288
Async XLA Ops:
  0.6 59.5 %copy-start = (f32[768,256]{1,0:T(8,128)S(1)}, f32[768,256]{1,0:T(8,128)}, u32[]{:S(2)}) copy-start(f32[768,256]{1,0:T(8,128)} %global_params.1) | copy-start | bytes 2359300

commit v4 on v3

--- a/solution.py
+++ b/solution.py
@@ -11,6 +11,7 @@
 ROWS = 768
 COLS = 256
 GROUP = 48
+LEVELS = 32767.0
 OWN = 6
 HALF = ROWS // 2
 MESH = pl.DeviceIdType.MESH
@@ -39,7 +40,7 @@
     tokens, query_weight, global_params, local_params, momentum, inner_steps, replica_tokens, plan,
     queries, residual, new_momentum,
     token_buf, weight_buf, global_buf, local_buf, momentum_buf, table_buf, term_buf, steps_buf, trained_buf,
-    got1, far_send, far_got, moment_send, moment_got, gathered,
+    got1, own_sum, far_send, far_got, step_send, step_got, moment_send, moment_got, gathered,
     load_sem, s1_send, s1_got, s2_send, s2_got, s3_send, s3_got, s4_send, s4_got, s5_send, s5_got,
     w_send, w_got, m_send, m_got,
 ):
@@ -172,13 +173,21 @@
     for (dy, index, dc), copy in reversed(list(zip(window, first))):
         copy.wait_recv()
         summed = summed + got1[8 * dy + 2 * index + dc].astype(jnp.float32)
-    far_send[...] = summed
+    own_sum[...] = summed
+    peak = jnp.max(jnp.max(jnp.abs(summed), axis=1, keepdims=True), axis=0, keepdims=True)
+    peak = jnp.maximum(peak, 1e-30)
+    far_send[...] = jnp.round(summed * (LEVELS / peak)).astype(jnp.int32).astype(jnp.int16)
+    step_send[...] = jnp.broadcast_to(peak * (1.0 / LEVELS), step_send.shape)
 
     def to_hub(index):
         return remote(far_send, far_got.at[index], s2_send, s2_got, index, (64 * y + kind, shard))
 
+    def step_to_hub(index):
+        return remote(step_send, step_got.at[index], s2_send, s2_got, index + 8, (64 * y + kind, shard))
+
     @pl.when(jnp.logical_not(hub))
     def _():
+        step_to_hub(ring).start()
         to_hub(ring).start()
 
     across_copy = remote(own_weight, weight_buf.at[shard], w_send, w_got, 4, (rep, across))
@@ -222,21 +231,30 @@
 
     @pl.when(hub)
     def _():
-        summed = far_send[...]
+        summed = own_sum[...]
         for index in (1, 2, 3, 7, 6, 5, 4):
+            step_to_hub(index).wait_recv()
             to_hub(index).wait_recv()
-            summed = summed + far_got[index]
+            summed = summed + far_got[index].astype(jnp.int32).astype(jnp.float32) * step_got[index, :1, :1]
         average = rotate(summed, table_buf[...])
         for index in range(8):
             moment_send[index] = average[OWN * index:OWN * (index + 1), :]
         own_global = global_buf[pl.ds(pl.multiple_of(group * GROUP, GROUP), GROUP), :]
         rest = (1.0 - keep) * (own_global - average)
         gathered[pl.ds(pl.multiple_of(group * GROUP, GROUP), GROUP), :] = rest.astype(jnp.bfloat16)
-        to_ring(1).start()
+        for index in (1, 7, 4):
+            to_ring(index).start()
+
+    after = jnp.where(ring < 4, ring + 1, ring - 1)
+    passes = jnp.logical_and(ring != 0, jnp.logical_and(ring != 3, jnp.logical_and(ring != 4, ring != 5)))
 
     @pl.when(jnp.logical_not(hub))
     def _():
         to_ring(ring).wait_recv()
+
+    @pl.when(passes)
+    def _():
+        to_ring(after).start()
 
     spot = lax.rem(z, 4)
     near = [(dy, step) for dy in (1, 0) for step in (2, 1, 3, 0)][:-1]
@@ -259,8 +277,6 @@
 
     @pl.when(hub)
     def _():
-        for index in (2, 3, 7, 4, 5, 6):
-            to_ring(index).start()
         for index in range(1, 8):
             to_owner(index).start()
 
@@ -307,11 +323,17 @@
     @pl.when(jnp.logical_not(hub))
     def _():
         to_hub(ring).wait_send()
+        step_to_hub(ring).wait_send()
+
+    @pl.when(passes)
+    def _():
+        to_ring(after).wait_send()
 
     @pl.when(hub)
     def _():
+        for index in (1, 7, 4):
+            to_ring(index).wait_send()
         for index in range(1, 8):
-            to_ring(index).wait_send()
             to_owner(index).wait_send()
 
         @pl.when(owner)
@@ -330,9 +352,9 @@
     queries, residual, new_momentum = pl.pallas_call(
         kernel,
         out_shape=(
-            jax.ShapeDtypeStruct((224, 128), bf16),
-            jax.ShapeDtypeStruct((ROWS, COLS), bf16),
-            jax.ShapeDtypeStruct((OWN, COLS), f32),
+            pltpu.VMEM((224, 128), bf16),
+            pltpu.VMEM((ROWS, COLS), bf16),
+            pltpu.VMEM((OWN, COLS), f32),
         ),
         in_specs=[hbm] * 7 + [smem],
         out_specs=(vmem, vmem, vmem),
@@ -348,13 +370,16 @@
             pltpu.VMEM((1, 128), jnp.int32),
             pltpu.VMEM((16, GROUP, COLS), bf16),
             pltpu.VMEM((GROUP, COLS), f32),
-            pltpu.VMEM((8, GROUP, COLS), f32),
+            pltpu.VMEM((GROUP, COLS), jnp.int16),
+            pltpu.VMEM((8, GROUP, COLS), jnp.int16),
+            pltpu.VMEM((8, BLOCK), f32),
+            pltpu.VMEM((8, 8, BLOCK), f32),
             pltpu.VMEM((8, OWN, COLS), f32),
             pltpu.VMEM((OWN, COLS), f32),
             pltpu.VMEM((ROWS, COLS), bf16),
             dma((7,)),
             dma((16,)), dma((16,)),
-            dma((8,)), dma((8,)),
+            dma((16,)), dma((16,)),
             dma((8,)), dma((8,)),
             dma((8,)), dma((8,)),
             dma((8,)), dma((8,)),

time: 65.1 us -> 56.9 us (0.87)
  the two profiles are of different devices: /device:TPU:257 before, /device:TPU:1 now
where the time goes in v4:
time: 56.9 us; the launch traced here: 56.3 us
  Pallas kernels  52.7 us (93%)
  between operations  1.37 us (2%)
  local copies, waits for them, and re-layouts  1.23 us (2%)
  other arithmetic  0.97 us (2%)
    pallas_call x1, Pallas kernels, local(): pl.pallas_call(kernel, out_shape=(pltpu.VMEM((224, 128), bf16), pltpu.VME...  52.7 us
    unnamed x4, local copies, waits for them, and re-layouts  1.23 us

profile of v4, /device:TPU:1, one launch (start us, length us, event | category | flops | bytes accessed | tf_op | source)
XLA Modules:
  0.0 56.3 jit_solution(7922786093296698856)
XLA Ops:
  0.6 0.0 copy-start
  1.4 52.7 %outer_step.1 = (bf16[224,128]{1,0:T(8,128)(2,1)S(1)}, bf16[768,256]{1,0:T(8,128)(2,1)S(1)}, f32[6,256]{1,0:T(8,128)S(1)}) custom-call(bf16[224,6144]{1,0:T(8,128)(2,1)} %tokens.1, bf16[1,768,128]{2,1,0:T(8,128)(2,1)} %query_weight.1, f32[768,256]{1,0:T(8,128)} %global_params.1, bf16[1,768,256]{2,1,0:T(8,128)(2,1)} %local_params.1, f32[6,8,256]{2,1,0:T(8,128)} %bitcast.3, ...), custom_call_target="tpu_custom_call" | custom-call | tf_op jit(solution)/shard_map/outer_step/pallas_call | solution.py:352
  54.1 0.6 %copy.13 = bf16[224,128]{1,0:T(8,128)(2,1)} copy(bf16[224,128]{1,0:T(8,128)(2,1)S(1)} %get-tuple-element.9) | data formatting | bytes 114688
  54.7 0.6 %copy.14 = f32[6,256]{1,0:T(8,128)} copy(f32[6,256]{1,0:T(8,128)S(1)} %get-tuple-element.11) | data formatting | bytes 12288
  55.3 0.0 copy-done
  55.3 1.0 %convert_add_fusion = f32[768,256]{1,0:T(8,128)} fusion(bf16[768,256]{1,0:T(8,128)(2,1)S(1)} %get-tuple-element.7, f32[768,256]{1,0:T(8,128)S(1)} %copy-done), kind=kLoop, calls=%fused_computation | loop fusion | flops 589824 | bytes 1966080 | tf_op jit(solution)/shard_map/add | solution.py:397
Async XLA Ops:
  0.6 54.7 %copy-start = (f32[768,256]{1,0:T(8,128)S(1)}, f32[768,256]{1,0:T(8,128)}, u32[]{:S(2)}) copy-start(f32[768,256]{1,0:T(8,128)} %global_params.1) | copy-start | bytes 2359300

commit v5 on v4

--- a/solution.py
+++ b/solution.py
@@ -39,10 +39,10 @@
 def kernel(
     tokens, query_weight, global_params, local_params, momentum, inner_steps, replica_tokens, plan,
     queries, residual, new_momentum,
-    token_buf, weight_buf, global_buf, local_buf, momentum_buf, table_buf, term_buf, steps_buf, trained_buf,
+    token_buf, weight_buf, global_buf, local_buf, momentum_buf, table_buf, term_buf, steps_buf, trained_buf, plan_buf,
     got1, own_sum, far_send, far_got, step_send, step_got, moment_send, moment_got, gathered,
     load_sem, s1_send, s1_got, s2_send, s2_got, s3_send, s3_got, s4_send, s4_got, s5_send, s5_got,
-    w_send, w_got, m_send, m_got,
+    w_send, w_got, m_send, m_got, told,
 ):
     rep, shard = lax.axis_index("rep"), lax.axis_index("fsdp")
     core = lax.rem(rep, 2)
@@ -67,16 +67,17 @@
     for index, (source, target) in enumerate((
         (local_params.at[0], local_buf), (global_params, global_buf), (momentum, momentum_buf),
         (query_weight.at[0], weight_buf.at[shard]), (tokens, token_buf),
-        (inner_steps, steps_buf), (replica_tokens, trained_buf),
+        (inner_steps, steps_buf), (replica_tokens, trained_buf), (plan, plan_buf),
     )):
         loads.append(pltpu.make_async_copy(source, target, load_sem.at[index]))
-        loads[-1].start()
+        if index < 2:
+            loads[-1].start()
 
     barrier = pltpu.get_barrier_semaphore()
     count = 0
-    for dy in (0, 1):
-        for dz in (0, 1, -1, 2, -2):
-            for dc in (0, 1):
+    for dz in (2, -2, 1, -1, 0):
+        for dy in (1, 0):
+            for dc in (1, 0):
                 if (dy, dz, dc) != (0, 0, 0):
                     pl.semaphore_signal(barrier, inc=1, device_id=(at(dy, dz, dc)[0], shard), device_id_type=MESH)
                     count += 1
@@ -86,8 +87,15 @@
 
     @pl.when(hub)
     def _():
-        for step in range(1, 8):
+        for step in (1, 2, 3, 5, 6, 7):
             pl.semaphore_signal(barrier, inc=1, device_id=(64 * y + 8 * step + kind, shard), device_id_type=MESH)
+
+    @pl.when(ring == 4)
+    def _():
+        pl.semaphore_signal(barrier, inc=1, device_id=(64 * y + 8 * 3 + kind, shard), device_id_type=MESH)
+
+    for index in (5, 6, 2, 7, 3, 4):
+        loads[index].start()
 
     row = lax.broadcasted_iota(jnp.int32, (BLOCK, BLOCK), 0)
     col = lax.broadcasted_iota(jnp.int32, (BLOCK, BLOCK), 1)
@@ -125,14 +133,22 @@
     lax.fori_loop(0, ROWS // 192, code_rows, 0)
 
     loads[2].wait()
-    fragment = lax.broadcasted_iota(jnp.int32, momentum_buf.shape, 1)
-    slot = jnp.sum(jnp.where(fragment == plan[0], momentum_buf[...], 0.0), axis=1)
+    loads[7].wait()
+    chosen = jnp.broadcast_to(plan_buf[...], (OWN, COLS))
+    slot = jnp.zeros((OWN, COLS), jnp.float32)
+    for fragment in range(8):
+        slot = slot + jnp.where(chosen == fragment, momentum_buf[:, fragment, :], 0.0)
     spread = jnp.concatenate([jnp.where(kind == index, slot, 0.0) for index in range(8)], axis=0)
     chunk_rows = pl.ds(pl.multiple_of(chunk * GROUP, GROUP), GROUP)
     shifted = term_buf[chunk_rows, :].astype(jnp.float32) + slot_share * rotate(spread, table_buf[...])
     term_buf[chunk_rows, :] = shifted.astype(jnp.bfloat16)
 
-    pl.semaphore_wait(barrier, count + jnp.where(hub, 0, 1))
+    from_hub = jnp.where(jnp.logical_or(hub, ring == 4), 0, 1)
+    pl.semaphore_wait(barrier, count + from_hub + jnp.where(ring == 3, 1, 0))
+
+    @pl.when(ring == 3)
+    def _():
+        pl.semaphore_signal(told, inc=1, device_id=(64 * y + 8 * 4 + kind, shard), device_id_type=MESH)
 
     def remote(source, target, sends, gots, index, device):
         return pltpu.make_async_remote_copy(
@@ -181,6 +197,10 @@
 
     def to_hub(index):
         return remote(far_send, far_got.at[index], s2_send, s2_got, index, (64 * y + kind, shard))
+
+    @pl.when(ring == 4)
+    def _():
+        pl.semaphore_wait(told, 1)
 
     def step_to_hub(index):
         return remote(step_send, step_got.at[index], s2_send, s2_got, index + 8, (64 * y + kind, shard))
@@ -346,7 +366,6 @@
 ):
     hbm = pl.BlockSpec(memory_space=pl.ANY)
     vmem = pl.BlockSpec(memory_space=pltpu.VMEM)
-    smem = pl.BlockSpec(memory_space=pltpu.SMEM)
     dma = pltpu.SemaphoreType.DMA
     f32, bf16 = jnp.float32, jnp.bfloat16
     queries, residual, new_momentum = pl.pallas_call(
@@ -356,7 +375,7 @@
             pltpu.VMEM((ROWS, COLS), bf16),
             pltpu.VMEM((OWN, COLS), f32),
         ),
-        in_specs=[hbm] * 7 + [smem],
+        in_specs=[hbm] * 8,
         out_specs=(vmem, vmem, vmem),
         scratch_shapes=[
             pltpu.VMEM((224, 6144), bf16),
@@ -368,6 +387,7 @@
             pltpu.VMEM((ROWS, COLS), bf16),
             pltpu.VMEM((1, 128), jnp.int32),
             pltpu.VMEM((1, 128), jnp.int32),
+            pltpu.VMEM((1, 1), jnp.int32),
             pltpu.VMEM((16, GROUP, COLS), bf16),
             pltpu.VMEM((GROUP, COLS), f32),
             pltpu.VMEM((GROUP, COLS), jnp.int16),
@@ -377,7 +397,7 @@
             pltpu.VMEM((8, OWN, COLS), f32),
             pltpu.VMEM((OWN, COLS), f32),
             pltpu.VMEM((ROWS, COLS), bf16),
-            dma((7,)),
+            dma((8,)),
             dma((16,)), dma((16,)),
             dma((16,)), dma((16,)),
             dma((8,)), dma((8,)),
@@ -385,6 +405,7 @@
             dma((8,)), dma((8,)),
             dma((9,)), dma((9,)),
             dma((8,)), dma(()),
+            pltpu.SemaphoreType.REGULAR,
         ],
         compiler_params=pltpu.CompilerParams(
             collective_id=0, has_side_effects=True, vmem_limit_bytes=60 * 1024 * 1024
@@ -392,7 +413,7 @@
         name="outer_step",
     )(
         tokens, query_weight, global_params, local_params, momentum.transpose(1, 0, 2),
-        inner_steps.reshape(1, 128), replica_tokens.reshape(1, 128), plan,
+        inner_steps.reshape(1, 128), replica_tokens.reshape(1, 128), plan.reshape(1, 1),
     )
     new_params = keep * global_params + residual.astype(f32)
     return queries, new_params, new_momentum

time: 56.9 us -> 55.9 us (0.982)
  Pallas kernels: 52.7 us -> 52.1 us
    pallas_call x1, Pallas kernels: 52.7 us -> 52.1 us  [local(): pl.pallas_call(kernel, out_shape=(pltpu.VMEM((224, 128), bf16), pltpu.VME...]
where the time goes in v5:
time: 55.9 us; the launch traced here: 55.7 us
  Pallas kernels  52.1 us (93%)
  between operations  1.37 us (2%)
  local copies, waits for them, and re-layouts  1.23 us (2%)
  other arithmetic  0.97 us (2%)
    pallas_call x1, Pallas kernels, local(): pl.pallas_call(kernel, out_shape=(pltpu.VMEM((224, 128), bf16), pltpu.VME...  52.1 us
    unnamed x4, local copies, waits for them, and re-layouts  1.23 us

profile of v5, /device:TPU:1, one launch (start us, length us, event | category | flops | bytes accessed | tf_op | source)
XLA Modules:
  0.0 55.7 jit_solution(9800250060637068491)
XLA Ops:
  0.6 0.0 copy-start
  1.4 52.1 %outer_step.1 = (bf16[224,128]{1,0:T(8,128)(2,1)S(1)}, bf16[768,256]{1,0:T(8,128)(2,1)S(1)}, f32[6,256]{1,0:T(8,128)S(1)}) custom-call(bf16[224,6144]{1,0:T(8,128)(2,1)} %tokens.1, bf16[1,768,128]{2,1,0:T(8,128)(2,1)} %query_weight.1, f32[768,256]{1,0:T(8,128)} %global_params.1, bf16[1,768,256]{2,1,0:T(8,128)(2,1)} %local_params.1, f32[6,8,256]{2,1,0:T(8,128)} %bitcast.5, ...), custom_call_target="tpu_custom_call" | custom-call | tf_op jit(solution)/shard_map/outer_step/pallas_call | solution.py:371
  53.5 0.6 %copy.13 = bf16[224,128]{1,0:T(8,128)(2,1)} copy(bf16[224,128]{1,0:T(8,128)(2,1)S(1)} %get-tuple-element.9) | data formatting | bytes 114688
  54.1 0.6 %copy.14 = f32[6,256]{1,0:T(8,128)} copy(f32[6,256]{1,0:T(8,128)S(1)} %get-tuple-element.11) | data formatting | bytes 12288
  54.7 0.0 copy-done
  54.7 1.0 %convert_add_fusion = f32[768,256]{1,0:T(8,128)} fusion(bf16[768,256]{1,0:T(8,128)(2,1)S(1)} %get-tuple-element.7, f32[768,256]{1,0:T(8,128)S(1)} %copy-done), kind=kLoop, calls=%fused_computation | loop fusion | flops 589824 | bytes 1966080 | tf_op jit(solution)/shard_map/add | solution.py:418
Async XLA Ops:
  0.6 54.1 %copy-start = (f32[768,256]{1,0:T(8,128)S(1)}, f32[768,256]{1,0:T(8,128)}, u32[]{:S(2)}) copy-start(f32[768,256]{1,0:T(8,128)} %global_params.1) | copy-start | bytes 2359300
